TPU v7x, 32 devices: a whole 2x2x4 slice. The times are simulated.
32 devices in a mesh: member: 2 (over x), lon: 16 (over z, y, core).
Axes of the slice: x: 2, y: 2, z: 4, core: 2. Of those that a mesh axis runs over, the one named last changes fastest.
Arguments:
- tracer_field: float32 [16, 2, 192, 768], P('member', None, 'lon'), parts along dimension 0, may hold values from -6 to 6
- courant_lon: float32 [4, 192, 768], P('member', 'lon'), parts along dimension 0, may hold values from -0.4 to 0.4
- courant_lat: float32 [4, 192, 768], P('member', 'lon'), parts along dimension 0, may hold values from -0.4 to 0.4
- diffusivity: float32 [2, 192, 768], P('member', 'lon'), parts along dimension 0, may hold values from 0.1 to 4
- polar_mask: int32 [768], replicated, may hold values from 0 to 1, as said below
- cutoff: int32 [768], replicated, may hold values from 4 to 95, as said below
Outputs:
- updated_field: float32 [16, 2, 192, 768], P('member', None, 'lon'), parts along dimension 0
There are 2 independent parts, one for each index of `member`. A program takes and returns all parts, laid end to end along the dimension named above; an argument that names none is the same for every part. Nothing has to cross between parts.
Inputs may be any that keep to these rules, and one draw needn't show every extreme that they name: `polar_mask`: 1 on the first 128 rows and on a last run of 64 to 128 rows, 0 elsewhere. `cutoff`: only rows with mask 1 use it.
All inputs are finite; a program needn't handle non-finite values.
Results may differ from a plain program's by a relative error of at most 0.00005.
Values sent between devices are 32-bit elements; how exact they have to be, the bound alone decides.
A program may use at most 128 MiB of HBM per device.

v0:
```python
import math
import jax
import jax.numpy as jnp
from jax import lax
from jax.sharding import PartitionSpec as P


def padded(x, sides, width):
    for axis, dim in sides:
        size, length = (lax.axis_size(axis), x.shape[dim])
        up = [(i, (i + 1) % size) for i in range(size)]
        down = [(j, i) for i, j in up]
        last = lax.slice_in_dim(x, length - width, length, axis=dim)
        leading = lax.slice_in_dim(x, 0, width, axis=dim)
        before = lax.ppermute(last, axis, up)
        after = lax.ppermute(leading, axis, down)
        x = jnp.concatenate([before, x, after], axis=dim)
    return x


def vertical_solve(diffusivity, field):
    levels = field.shape[1]
    zeros_plane = jnp.zeros_like(diffusivity[0])
    upper_list = []
    rhs_list = []
    prev_upper = None
    prev_rhs = None
    for lev_index in range(levels):
        below = diffusivity[lev_index - 1] if lev_index > 0 else zeros_plane
        above = diffusivity[lev_index] if lev_index < levels - 1 else zeros_plane
        diagonal = 1.0 + below + above
        source = field[:, lev_index]
        if lev_index == 0:
            denom = diagonal
            new_rhs = source / denom
        else:
            denom = diagonal + below * prev_upper
            new_rhs = (source + below * prev_rhs) / denom
        new_upper = -above / denom
        upper_list.append(new_upper)
        rhs_list.append(new_rhs)
        prev_upper = new_upper
        prev_rhs = new_rhs
    result = [None] * levels
    current = rhs_list[levels - 1]
    result[levels - 1] = current
    lev_index = 0
    current = rhs_list[lev_index] - upper_list[lev_index] * current
    result[lev_index] = current
    return jnp.stack(result, axis=1)


def fourier_tables(length):
    half_len = length // 2
    column = jnp.arange(length, dtype=jnp.int32)[:, None]
    wavenum = jnp.arange(1, half_len + 1, dtype=jnp.int32)[None, :]
    phase = column * wavenum % length
    angle = 2.0 * math.pi / length * phase.astype(jnp.float32)
    return (jnp.cos(angle), jnp.sin(angle))


def high_part(block, row_cut, cosine, sine):
    length = block.shape[1]
    half_len = length // 2
    highest = lax.Precision.HIGHEST
    real_part = jnp.einsum("bir,im->brm", block, cosine, precision=highest)
    imag_part = jnp.einsum("bir,im->brm", block, sine, precision=highest)
    wavenum = jnp.arange(1, half_len + 1, dtype=jnp.int32)
    weights = jnp.where(wavenum == half_len, 1.0 / length, 2.0 / length).astype(jnp.float32)
    keeper = jnp.where(wavenum[None, :] > row_cut[:, None], weights[None, :], 0.0)
    return jnp.einsum(
        "brm,im->bir", real_part * keeper[None], cosine, precision=highest
    ) + jnp.einsum("brm,im->bir", imag_part * keeper[None], sine, precision=highest)


def local(tracer_field, courant_lon, courant_lat, diffusivity, polar_mask, cutoff):
    tracers, levels, lon_local, lat_rows = tracer_field.shape
    zero_row = jnp.zeros_like(tracer_field[..., :1])
    north_next = jnp.concatenate([tracer_field[..., 1:], zero_row], axis=3)
    north = (
        jnp.maximum(courant_lat, 0.0)[None] * tracer_field
        + jnp.minimum(courant_lat, 0.0)[None] * north_next
    )
    south = jnp.concatenate([zero_row, north[..., :-1]], axis=3)
    stacked = jnp.concatenate([tracer_field, courant_lon[None]], axis=0)
    extended = padded(stacked, (("lon", 2),), 1)
    tracer_ext = extended[:tracers]
    speed_ext = extended[tracers][None, :, :-1]
    east_all = (
        jnp.maximum(speed_ext, 0.0) * tracer_ext[:, :, :-1]
        + jnp.minimum(speed_ext, 0.0) * tracer_ext[:, :, 1:]
    )
    east = east_all[:, :, 1:]
    west = east_all[:, :, :-1]
    advected = tracer_field - (east - west) - (north - south)
    batched = advected.reshape(tracers * levels, lon_local, lat_rows)
    length = lon_local * lax.axis_size("lon")
    cosine, sine = fourier_tables(length)
    mask_float = polar_mask.astype(jnp.float32)
    row_count = lat_rows // lax.axis_size("lon")
    first_row = lax.axis_index("lon") * row_count
    my_cut = lax.dynamic_slice_in_dim(cutoff, first_row, row_count)
    my_mask = lax.dynamic_slice_in_dim(mask_float, first_row, row_count)
    removed = (
        high_part(
            lax.all_to_all(batched, "lon", split_axis=2, concat_axis=1, tiled=True),
            my_cut,
            cosine,
            sine,
        )
        * my_mask[None, None, :]
    )
    correction = lax.all_to_all(removed, "lon", split_axis=1, concat_axis=2, tiled=True)
    filtered = (batched - correction).reshape(tracers, levels, lon_local, lat_rows)
    return vertical_solve(diffusivity, filtered)


def solution(mesh):
    placed = (
        P("member", None, "lon", None),
        P("member", "lon", None),
        P("member", "lon", None),
        P("member", "lon", None),
        P(),
        P(),
    )
    return jax.shard_map(
        local, mesh=mesh, in_specs=placed, out_specs=P("member", None, "lon", None), check_vma=False
    )
```

profile of v0, /device:TPU:0, one launch (start us, length us, event | category | flops | bytes accessed | tf_op | source)
XLA Modules:
  0.0 89.5 jit_solution(6929786615368778992)
XLA Ops:
  0.0 0.0 copy-start.5
  0.0 0.0 copy-start
  0.0 1.0 %pad_maximum_fusion.9 = (f32[9,2,1,768]{3,1,0,2:T(2,128)S(1)}, f32[9,2,1,768]{3,1,0,2:T(2,128)S(1)}) fusion(f32[1,2,12,768]{3,1,0,2:T(2,128)} %bitcast.52, f32[8,2,12,768]{3,1,2,0:T(2,128)} %param.6), kind=kLoop, calls=%fused_computation.42 | loop fusion | flops 27648 | bytes 774144 | tf_op jit(solution)/shard_map/slice | solution.py:13
  1.0 0.5 collective-permute-start
  1.5 5.1 %collective-permute-start.1 = (f32[9,2,1,768]{3,1,0,2:T(2,128)S(1)}, f32[9,2,1,768]{3,1,0,2:T(2,128)S(1)}, u32[]{:S(2)}, u32[]{:S(2)}) collective-permute-start(f32[9,2,1,768]{3,1,0,2:T(2,128)S(1)} %get-tuple-element.10), channel_id=1, source_target_pairs={{1,0},{2,1},{3,2},{4,3},{5,4},{6,5},{7,6},{8,7},{9,8},{10,9},{11,1... | collective-permute-start | bytes 165896 | tf_op jit(solution)/shard_map/ppermute | solution.py:16
  6.5 1.7 %slice.56 = f32[8,2,12,767]{3,1,2,0:T(2,128)S(1)} slice(f32[8,2,12,768]{3,1,2,0:T(2,128)} %param.6), slice={[0:8], [0:2], [0:12], [1:768]} | slice | bytes 1178112 | tf_op jit(solution)/shard_map/slice | solution.py:79
  8.3 0.0 copy-done.5
  8.3 0.1 broadcast_maximum_fusion
  8.4 0.0 copy-start.3
  8.4 0.1 copy.45
  8.4 0.0 copy-done
  8.5 0.4 multiply_add_fusion
  8.9 0.0 collective-permute-done
  8.9 0.0 collective-permute-done.1
  8.9 0.3 copy-done.3
  9.3 0.1 slice_maximum_fusion
  9.4 0.4 fusion.3
  9.8 0.8 fusion.6
  10.5 0.0 copy-start.1
  10.6 0.4 reshape.61
  11.0 5.0 %copy.19 = f32[16,12,768]{0,1,2:T(8,128)} copy(f32[16,12,768]{2,0,1:T(8,128)S(1)} %reshape.61) | data formatting | bytes 1179648 | tf_op jit(solution)/shard_map/reshape | solution.py:96
  16.0 0.0 copy-done.1
  16.0 0.0 copy-start.6
  16.0 5.5 %reshape.64 = f32[16,1,9216]{2,1,0:T(1,128)} reshape(f32[768,12,16]{2,1,0:T(8,128)} %bitcast.46) | data formatting | bytes 1179648
  21.4 5.0 %all-to-all-start = ((f32[16,1,9216]{2,1,0:T(1,128)}), f32[16,1,9216]{2,1,0:T(1,128)S(1)}, u32[]{:S(2)}, u32[]{:S(2)}) async-start(f32[16,1,9216]{2,1,0:T(1,128)} %reshape.64), calls=%async_computation | async-start | bytes 1179648 | tf_op jit(solution)/shard_map/all_to_all | solution.py:106
  26.4 0.0 copy-done.6
  26.4 0.8 dynamic_slice.6
  27.2 0.1 dynamic_slice.7
  27.3 0.1 compare_select_fusion
  27.4 14.6 %all-to-all-done = f32[16,1,9216]{2,1,0:T(1,128)S(1)} async-done(((f32[16,1,9216]{2,1,0:T(1,128)}), f32[16,1,9216]{2,1,0:T(1,128)S(1)}, u32[]{:S(2)}, u32[]{:S(2)}) %all-to-all-start) | async-done | bytes 589856 | tf_op jit(solution)/shard_map/all_to_all | solution.py:106
  42.0 0.5 broadcast.105
  42.5 1.9 %reduce = f32[16,9216]{1,0:T(8,128)S(1)} reduce(f32[16,1,9216]{2,1,0:T(1,128)S(1)} %all-to-all-done, f32[]{:T(128)} %broadcast.105), dimensions={1}, to_apply=%all_to_all.26.reduce_sub_computation | reduce | bytes 1179652 | tf_op jit(solution)/shard_map/all_to_all | solution.py:106
  44.4 4.4 %reshape.65 = f32[768,12,16]{2,1,0:T(8,128)} reshape(f32[16,9216]{1,0:T(8,128)S(1)} %reduce) | data formatting | bytes 1179648
  48.8 4.7 %copy.21 = f32[16,16,12,48]{3,0,2,1:T(8,128)S(1)} copy(f32[16,16,12,48]{0,2,3,1:T(8,128)} %bitcast.47) | data formatting | bytes 1179648 | tf_op jit(solution)/shard_map/all_to_all | solution.py:106
  53.5 0.8 copy.22
  54.3 1.2 %convolution_multiply_fusion.1 = f32[16,48,96]{2,1,0:T(8,128)S(1)} fusion(f32[16,192,48]{1,2,0:T(8,128)S(1)} %copy.22, f32[48,96]{1,0:T(8,128)S(1)} %compare_select_fusion, s32[96]{0:T(128)S(1)} %iota_add_fusion), kind=kOutput, calls=%fused_computation.4 | convolution fusion | flops 170108928 | bytes 903552 | tf_op jit(solution)/shard_map/bir,im->brm/dot_general | solution.py:66
  55.4 1.2 %convolution_multiply_fusion = f32[16,48,96]{2,1,0:T(8,128)S(1)} fusion(f32[16,192,48]{1,2,0:T(8,128)S(1)} %copy.22, f32[48,96]{1,0:T(8,128)S(1)} %compare_select_fusion, s32[96]{0:T(128)S(1)} %iota_add_fusion), kind=kOutput, calls=%fused_computation.3 | convolution fusion | flops 170108928 | bytes 903552 | tf_op jit(solution)/shard_map/bir,im->brm/dot_general | solution.py:67
  56.6 1.2 %fusion.12 = f32[192,16,48]{0,2,1:T(8,128)S(1)} fusion(f32[16,48,96]{2,1,0:T(8,128)S(1)} %convolution_multiply_fusion.1, s32[96]{0:T(128)S(1)} %iota_add_fusion), kind=kOutput, calls=%fused_computation.26 | convolution fusion | flops 170035200 | bytes 885120 | tf_op jit(solution)/shard_map/brm,im->bir/dot_general | solution.py:71
  57.8 1.2 %fusion.1 = f32[16,192,48]{1,2,0:T(8,128)S(1)} fusion(f32[192,16,48]{0,2,1:T(8,128)S(1)} %fusion.12, f32[16,48,96]{2,1,0:T(8,128)S(1)} %convolution_multiply_fusion, f32[48]{0:T(128)S(1)} %dynamic_slice.7, s32[96]{0:T(128)S(1)} %iota_add_fusion), kind=kOutput, calls=%fused_computation.2 | convolution fusion | flops 170330112 | bytes 1475136 | tf_op jit(solution)/shard_map/brm,im->bir/dot_general | solution.py:73
  58.9 0.8 copy.24
  59.8 0.0 copy-start.4
  59.8 2.4 %reshape.66 = f32[16,1,9216]{2,1,0:T(1,128)} reshape(f32[192,16,48]{2,1,0:T(8,128)S(1)} %bitcast.48) | data formatting | bytes 1179648
  62.2 4.4 %all-to-all-start.1 = ((f32[16,1,9216]{2,1,0:T(1,128)}), f32[16,1,9216]{2,1,0:T(1,128)S(1)}, u32[]{:S(2)}, u32[]{:S(2)}) async-start(f32[16,1,9216]{2,1,0:T(1,128)} %reshape.66), calls=%async_computation.1 | async-start | bytes 1179648 | tf_op jit(solution)/shard_map/all_to_all | solution.py:113
  66.6 0.0 copy-done.4
  66.6 0.1 multiply_add_fusion.1
  66.7 15.4 %all-to-all-done.1 = f32[16,1,9216]{2,1,0:T(1,128)S(1)} async-done(((f32[16,1,9216]{2,1,0:T(1,128)}), f32[16,1,9216]{2,1,0:T(1,128)S(1)}, u32[]{:S(2)}, u32[]{:S(2)}) %all-to-all-start.1) | async-done | bytes 589856 | tf_op jit(solution)/shard_map/all_to_all | solution.py:113
  82.2 2.0 %reduce.1 = f32[16,9216]{1,0:T(8,128)S(1)} reduce(f32[16,1,9216]{2,1,0:T(1,128)S(1)} %all-to-all-done.1, f32[]{:T(128)} %broadcast.105), dimensions={1}, to_apply=%all_to_all.30.reduce_sub_computation | reduce | bytes 1179652 | tf_op jit(solution)/shard_map/all_to_all | solution.py:113
  84.1 0.7 reshape.67
  84.8 0.9 %copy.25 = f32[16,12,16,48]{3,2,0,1:T(8,128)S(1)} copy(f32[16,12,16,48]{3,0,1,2:T(8,128)S(1)} %bitcast.49) | data formatting | bytes 1179648 | tf_op jit(solution)/shard_map/all_to_all | solution.py:113
  85.7 0.0 copy-start.2
  85.7 1.3 %all_to_all.33 = f32[8,2,12,768]{3,1,0,2:T(2,128)S(1)} reshape(f32[16,12,16,48]{3,2,0,1:T(8,128)S(1)} %copy.25) | data formatting | bytes 1179648 | tf_op jit(solution)/shard_map/all_to_all | solution.py:113
  87.1 0.0 copy-done.2
  87.1 0.3 sub.24
  87.4 0.7 multiply_subtract_fusion
  88.0 0.5 pad_maximum_fusion.4
  88.6 0.9 copy.26
  (6 shorter events, 0.1 us)
Async XLA Ops:
  0.0 8.3 %copy-start.5 = (f32[2,12,768]{2,0,1:T(2,128)S(1)}, f32[2,12,768]{2,0,1:T(2,128)}, u32[]{:S(2)}) copy-start(f32[2,12,768]{2,0,1:T(2,128)} %param.8) | copy-start | bytes 221188
  0.0 8.4 %copy-start = (f32[8,2,12,768]{3,1,2,0:T(2,128)S(1)}, f32[8,2,12,768]{3,1,2,0:T(2,128)}, u32[]{:S(2)}) copy-start(f32[8,2,12,768]{3,1,2,0:T(2,128)} %param.6) | copy-start | bytes 1769476
  1.0 7.9 %collective-permute-start = (f32[9,2,1,768]{3,1,0,2:T(2,128)S(1)}, f32[9,2,1,768]{3,1,0,2:T(2,128)S(1)}, u32[]{:S(2)}, u32[]{:S(2)}) collective-permute-start(f32[9,2,1,768]{3,1,0,2:T(2,128)S(1)} %get-tuple-element.9), channel_id=1, source_target_pairs={{0,1},{1,2},{2,3},{3,4},{4,5},{5,6},{6,7},{7,8},{8,9},{9,10},{10,1... | collective-permute-start | bytes 165896 | tf_op jit(solution)/shard_map/ppermute | solution.py:15
  1.5 7.4 %collective-permute-start.1 = (f32[9,2,1,768]{3,1,0,2:T(2,128)S(1)}, f32[9,2,1,768]{3,1,0,2:T(2,128)S(1)}, u32[]{:S(2)}, u32[]{:S(2)}) collective-permute-start(f32[9,2,1,768]{3,1,0,2:T(2,128)S(1)} %get-tuple-element.10), channel_id=1, source_target_pairs={{1,0},{2,1},{3,2},{4,3},{5,4},{6,5},{7,6},{8,7},{9,8},{10,9},{11,1... | collective-permute-start | bytes 165896 | tf_op jit(solution)/shard_map/ppermute | solution.py:16
  8.4 0.9 copy-start.3
  10.5 5.4 %copy-start.1 = (f32[8,2,12,768]{3,1,0,2:T(2,128)}, f32[8,2,12,768]{3,1,0,2:T(2,128)S(1)}, u32[]{:S(2)}) copy-start(f32[8,2,12,768]{3,1,0,2:T(2,128)S(1)} %fusion.6) | copy-start | bytes 1769476
  16.0 10.5 %copy-start.6 = (s32[768]{0:T(1024)S(1)}, s32[768]{0:T(1024)}, u32[]{:S(2)}) copy-start(s32[768]{0:T(1024)} %param.10) | copy-start | bytes 9220
  21.4 20.5 %all-to-all-start = ((f32[16,1,9216]{2,1,0:T(1,128)}), f32[16,1,9216]{2,1,0:T(1,128)S(1)}, u32[]{:S(2)}, u32[]{:S(2)}) async-start(f32[16,1,9216]{2,1,0:T(1,128)} %reshape.64), calls=%async_computation | async-start | bytes 1179648 | tf_op jit(solution)/shard_map/all_to_all | solution.py:106
  59.8 6.8 %copy-start.4 = (f32[1,12,768]{2,0,1:T(1,128)S(1)}, f32[1,12,768]{2,0,1:T(1,128)}, u32[]{:S(2)}) copy-start(f32[1,12,768]{2,0,1:T(1,128)} %param.9) | copy-start | bytes 110596
  62.2 20.0 %all-to-all-start.1 = ((f32[16,1,9216]{2,1,0:T(1,128)}), f32[16,1,9216]{2,1,0:T(1,128)S(1)}, u32[]{:S(2)}, u32[]{:S(2)}) async-start(f32[16,1,9216]{2,1,0:T(1,128)} %reshape.66), calls=%async_computation.1 | async-start | bytes 1179648 | tf_op jit(solution)/shard_map/all_to_all | solution.py:113
  85.7 1.3 %copy-start.2 = (f32[8,2,12,768]{3,1,0,2:T(2,128)S(1)}, f32[8,2,12,768]{3,1,0,2:T(2,128)}, u32[]{:S(2)}) copy-start(f32[8,2,12,768]{3,1,0,2:T(2,128)} %copy-done.1) | copy-start | bytes 1769476
where the time goes:
time: 90 us; the launch traced here: 89.5 us
  local copies, waits for them, and re-layouts  31.3 us (35%)
  waiting for transfers between devices  30 us (33%)
  starting transfers between devices  15 us (17%)
  other arithmetic  8.27 us (9%)
  matrix products  4.66 us (5%)
    all_to_all x1, waiting for transfers between devices, local(): lax.all_to_all(removed, 'lon', split_axis=1, concat_axis=2, tiled=True)  15.4 us
    all_to_all x1, waiting for transfers between devices, local(): lax.all_to_all(batched, 'lon', split_axis=2, concat_axis=1, tiled=True)  14.6 us
    unnamed x21, local copies, waits for them, and re-layouts  13.4 us
    all_to_all x3, local copies, waits for them, and re-layouts, local(): lax.all_to_all(batched, 'lon', split_axis=2, concat_axis=1, tiled=True)  5.92 us
    reshape x2, local copies, waits for them, and re-layouts, local(): batched = advected.reshape(tracers * levels, lon_local, lat_rows)  5.38 us
    ppermute x1, starting transfers between devices, padded(): after = lax.ppermute(leading, axis, down)  5.06 us
    all_to_all x1, starting transfers between devices, local(): lax.all_to_all(batched, 'lon', split_axis=2, concat_axis=1, tiled=True)  4.97 us
    all_to_all x1, starting transfers between devices, local(): lax.all_to_all(removed, 'lon', split_axis=1, concat_axis=2, tiled=True)  4.43 us
  transfers between devices with their start and end apart: 4, of which 2 were waited for; matrix products, arithmetic and copies ran while one was open for 4% of the time, Pallas kernels for 0%

commit v1 on v0

--- a/solution.py
+++ b/solution.py
@@ -103,7 +103,12 @@
     my_mask = lax.dynamic_slice_in_dim(mask_float, first_row, row_count)
     removed = (
         high_part(
-            lax.all_to_all(batched, "lon", split_axis=2, concat_axis=1, tiled=True),
+            jnp.concatenate(
+                lax.all_to_all(
+                    jnp.stack(jnp.split(batched, lax.axis_size("lon"), axis=2)), "lon", 0, 0
+                ),
+                axis=1,
+            ),
             my_cut,
             cosine,
             sine,

time: 90 us -> 75 us (0.83)
  local copies, waits for them, and re-layouts: 31.3 us -> 16.1 us
    unnamed x21 -> x36, local copies, waits for them, and re-layouts: 13.4 us -> 7.7 us
    all_to_all x3 -> x1, local copies, waits for them, and re-layouts: 5.92 us -> 0.57 us  [local(): lax.all_to_all(jnp.stack(jnp.split(batched, lax.axis_size('lon'), axis=2)...]
    reshape x2 -> x1, local copies, waits for them, and re-layouts: 5.38 us -> 0.41 us  [local(): batched = advected.reshape(tracers * levels, lon_local, lat_rows)]
where the time goes in v1:
time: 75 us; the launch traced here: 74.5 us
  waiting for transfers between devices  30 us (40%)
  local copies, waits for them, and re-layouts  16.1 us (21%)
  starting transfers between devices  15 us (20%)
  other arithmetic  8.4 us (11%)
  matrix products  4.66 us (6%)
    all_to_all x1, waiting for transfers between devices, local(): lax.all_to_all(removed, 'lon', split_axis=1, concat_axis=2, tiled=True)  15.4 us
    all_to_all x1, waiting for transfers between devices, local(): lax.all_to_all(jnp.stack(jnp.split(batched, lax.axis_size('lon'), axis=2)...  14.6 us
    unnamed x36, local copies, waits for them, and re-layouts  7.7 us
    ppermute x1, starting transfers between devices, padded(): after = lax.ppermute(leading, axis, down)  5.06 us
    all_to_all x1, starting transfers between devices, local(): lax.all_to_all(jnp.stack(jnp.split(batched, lax.axis_size('lon'), axis=2)...  4.97 us
    all_to_all x1, starting transfers between devices, local(): lax.all_to_all(removed, 'lon', split_axis=1, concat_axis=2, tiled=True)  4.43 us
    all_to_all x2, local copies, waits for them, and re-layouts, local(): lax.all_to_all(removed, 'lon', split_axis=1, concat_axis=2, tiled=True)  2.25 us
    all_to_all x1, other arithmetic, local(): lax.all_to_all(removed, 'lon', split_axis=1, concat_axis=2, tiled=True)  2.01 us
  transfers between devices with their start and end apart: 4, of which 2 were waited for; matrix products, arithmetic and copies ran while one was open for 4% of the time, Pallas kernels for 0%

profile of v1, /device:TPU:0, one launch (start us, length us, event | category | flops | bytes accessed | tf_op | source)
XLA Modules:
  0.0 74.5 jit_solution(2181363217038815638)
XLA Ops:
  0.0 1.0 %pad_maximum_fusion.9 = (f32[9,2,1,768]{3,1,0,2:T(2,128)S(1)}, f32[9,2,1,768]{3,1,0,2:T(2,128)S(1)}) fusion(f32[1,2,12,768]{3,1,0,2:T(2,128)} %bitcast.113, f32[8,2,12,768]{3,1,2,0:T(2,128)} %param.6), kind=kLoop, calls=%fused_computation.74 | loop fusion | flops 27648 | bytes 774144 | tf_op jit(solution)/shard_map/slice | solution.py:13
  1.0 0.5 collective-permute-start
  1.5 5.1 %collective-permute-start.1 = (f32[9,2,1,768]{3,1,0,2:T(2,128)S(1)}, f32[9,2,1,768]{3,1,0,2:T(2,128)S(1)}, u32[]{:S(2)}, u32[]{:S(2)}) collective-permute-start(f32[9,2,1,768]{3,1,0,2:T(2,128)S(1)} %get-tuple-element.10), channel_id=1, source_target_pairs={{1,0},{2,1},{3,2},{4,3},{5,4},{6,5},{7,6},{8,7},{9,8},{10,9},{11,1... | collective-permute-start | bytes 165896 | tf_op jit(solution)/shard_map/ppermute | solution.py:16
  6.5 1.7 %slice.56 = f32[8,2,12,767]{3,1,2,0:T(2,128)S(1)} slice(f32[8,2,12,768]{3,1,2,0:T(2,128)} %param.6), slice={[0:8], [0:2], [0:12], [1:768]} | slice | bytes 1178112 | tf_op jit(solution)/shard_map/slice | solution.py:79
  8.3 0.0 copy-done.5
  8.3 0.1 broadcast_maximum_fusion
  8.4 0.0 copy-start.3
  8.4 0.1 copy.39
  8.4 0.0 copy-done
  8.5 0.4 multiply_add_fusion
  8.9 0.0 collective-permute-done
  8.9 0.0 collective-permute-done.1
  8.9 0.3 copy-done.3
  9.3 0.1 slice_maximum_fusion
  9.4 0.4 fusion.3
  9.8 0.8 %fusion.6 = f32[8,2,12,768]{3,1,0,2:T(2,128)S(1)} fusion(f32[8,2,13,768]{3,1,0,2:T(2,128)S(1)} %fusion.3, f32[8,2,12,768]{3,1,0,2:T(2,128)S(1)} %multiply_add_fusion, f32[8,2,12,767]{3,1,0,2:T(2,128)S(1)} %bitcast.111, f32[8,2,12,768]{3,1,2,0:T(2,128)S(1)} %copy-done), kind=kLoop, calls=%fused_computation.14 | loop fusion | flops 589824 | bytes 3538176 | tf_op jit(solution)/shard_map/sub | solution.py:95
  10.5 0.0 copy-start.1
  10.6 0.4 reshape.67
  11.0 0.1 fusion.24
  11.1 0.1 fusion.23
  11.2 0.1 fusion.22
  11.3 0.1 fusion.21
  11.4 0.1 fusion.20
  11.5 0.1 fusion.19
  11.6 0.1 fusion.18
  11.7 0.1 fusion.16
  11.8 0.0 copy-done.1
  11.8 0.1 fusion.15
  11.9 0.1 fusion.14
  12.0 0.1 fusion.13
  12.0 0.1 fusion.12
  12.1 0.1 fusion.11
  12.2 0.1 fusion.10
  12.3 0.0 copy-start.6
  12.3 2.4 %reshape.72 = f32[16,1,9216]{2,1,0:T(1,128)} reshape(f32[16,12,16,48]{3,2,1,0:T(8,128)S(1)} %bitcast.112) | data formatting | bytes 1179648
  14.7 5.0 %all-to-all-start = ((f32[16,1,9216]{2,1,0:T(1,128)}), f32[16,1,9216]{2,1,0:T(1,128)S(1)}, u32[]{:S(2)}, u32[]{:S(2)}) async-start(f32[16,1,9216]{2,1,0:T(1,128)} %reshape.72), calls=%async_computation | async-start | bytes 1179648 | tf_op jit(solution)/shard_map/all_to_all | solution.py:107
  19.7 0.0 copy-done.6
  19.7 0.8 %dynamic_slice.6 = s32[48]{0:T(128)S(1)} dynamic-slice(s32[768]{0:T(1024)} %param.11, s32[]{:T(128)S(6)} %select_n.34), dynamic_slice_sizes={48} | dynamic-slice | bytes 388 | tf_op jit(solution)/shard_map/dynamic_slice | solution.py:102
  20.5 0.1 dynamic_slice.7
  20.6 0.1 compare_select_fusion
  20.6 14.6 %all-to-all-done = f32[16,1,9216]{2,1,0:T(1,128)S(1)} async-done(((f32[16,1,9216]{2,1,0:T(1,128)}), f32[16,1,9216]{2,1,0:T(1,128)S(1)}, u32[]{:S(2)}, u32[]{:S(2)}) %all-to-all-start) | async-done | bytes 589856 | tf_op jit(solution)/shard_map/all_to_all | solution.py:107
  35.2 0.6 broadcast.105
  35.8 2.0 %reduce = f32[16,9216]{1,0:T(8,128)S(1)} reduce(f32[16,1,9216]{2,1,0:T(1,128)S(1)} %all-to-all-done, f32[]{:T(128)} %broadcast.105), dimensions={1}, to_apply=%all_to_all.16.reduce_sub_computation | reduce | bytes 1179652 | tf_op jit(solution)/shard_map/all_to_all | solution.py:107
  37.8 0.7 reshape.73
  38.5 0.8 %copy.18 = f32[16,192,48]{1,2,0:T(8,128)S(1)} copy(f32[16,192,48]{2,0,1:T(8,128)S(1)} %bitcast.108) | data formatting | bytes 1179648 | tf_op jit(solution)/shard_map/reshape | solution.py:106
  39.3 1.2 %convolution_multiply_fusion.1 = f32[16,48,96]{2,1,0:T(8,128)S(1)} fusion(f32[16,192,48]{1,2,0:T(8,128)S(1)} %copy.18, f32[48,96]{1,0:T(8,128)S(1)} %compare_select_fusion, s32[96]{0:T(128)S(1)} %iota_add_fusion), kind=kOutput, calls=%fused_computation.4 | convolution fusion | flops 170108928 | bytes 903552 | tf_op jit(solution)/shard_map/bir,im->brm/dot_general | solution.py:66
  40.4 1.2 %convolution_multiply_fusion = f32[16,48,96]{2,1,0:T(8,128)S(1)} fusion(f32[16,192,48]{1,2,0:T(8,128)S(1)} %copy.18, f32[48,96]{1,0:T(8,128)S(1)} %compare_select_fusion, s32[96]{0:T(128)S(1)} %iota_add_fusion), kind=kOutput, calls=%fused_computation.3 | convolution fusion | flops 170108928 | bytes 903552 | tf_op jit(solution)/shard_map/bir,im->brm/dot_general | solution.py:67
  41.6 1.2 %fusion.28 = f32[192,16,48]{0,2,1:T(8,128)S(1)} fusion(f32[16,48,96]{2,1,0:T(8,128)S(1)} %convolution_multiply_fusion.1, s32[96]{0:T(128)S(1)} %iota_add_fusion), kind=kOutput, calls=%fused_computation.58 | convolution fusion | flops 170035200 | bytes 885120 | tf_op jit(solution)/shard_map/brm,im->bir/dot_general | solution.py:71
  42.8 1.2 %fusion.1 = f32[16,192,48]{1,2,0:T(8,128)S(1)} fusion(f32[192,16,48]{0,2,1:T(8,128)S(1)} %fusion.28, f32[16,48,96]{2,1,0:T(8,128)S(1)} %convolution_multiply_fusion, f32[48]{0:T(128)S(1)} %dynamic_slice.7, s32[96]{0:T(128)S(1)} %iota_add_fusion), kind=kOutput, calls=%fused_computation.2 | convolution fusion | flops 170330112 | bytes 1475136 | tf_op jit(solution)/shard_map/brm,im->bir/dot_general | solution.py:73
  44.0 0.8 %copy.20 = f32[16,192,48]{2,0,1:T(8,128)S(1)} copy(f32[16,192,48]{1,2,0:T(8,128)S(1)} %fusion.1) | data formatting | bytes 1179648 | tf_op jit(solution)/shard_map/mul | solution.py:105
  44.8 0.0 copy-start.4
  44.8 2.4 %reshape.74 = f32[16,1,9216]{2,1,0:T(1,128)} reshape(f32[192,16,48]{2,1,0:T(8,128)S(1)} %bitcast.109) | data formatting | bytes 1179648
  47.2 4.4 %all-to-all-start.1 = ((f32[16,1,9216]{2,1,0:T(1,128)}), f32[16,1,9216]{2,1,0:T(1,128)S(1)}, u32[]{:S(2)}, u32[]{:S(2)}) async-start(f32[16,1,9216]{2,1,0:T(1,128)} %reshape.74), calls=%async_computation.1 | async-start | bytes 1179648 | tf_op jit(solution)/shard_map/all_to_all | solution.py:118
  51.6 0.1 multiply_add_fusion.1
  51.8 15.4 %all-to-all-done.1 = f32[16,1,9216]{2,1,0:T(1,128)S(1)} async-done(((f32[16,1,9216]{2,1,0:T(1,128)}), f32[16,1,9216]{2,1,0:T(1,128)S(1)}, u32[]{:S(2)}, u32[]{:S(2)}) %all-to-all-start.1) | async-done | bytes 589856 | tf_op jit(solution)/shard_map/all_to_all | solution.py:118
  67.2 2.0 %reduce.1 = f32[16,9216]{1,0:T(8,128)S(1)} reduce(f32[16,1,9216]{2,1,0:T(1,128)S(1)} %all-to-all-done.1, f32[]{:T(128)} %broadcast.105), dimensions={1}, to_apply=%all_to_all.17.reduce_sub_computation | reduce | bytes 1179652 | tf_op jit(solution)/shard_map/all_to_all | solution.py:118
  69.2 0.7 reshape.75
  69.9 0.9 %copy.21 = f32[16,12,16,48]{3,2,0,1:T(8,128)S(1)} copy(f32[16,12,16,48]{3,0,1,2:T(8,128)S(1)} %bitcast.110) | data formatting | bytes 1179648 | tf_op jit(solution)/shard_map/all_to_all | solution.py:118
  70.8 0.0 copy-start.2
  70.8 1.3 %all_to_all.20 = f32[8,2,12,768]{3,1,0,2:T(2,128)S(1)} reshape(f32[16,12,16,48]{3,2,0,1:T(8,128)S(1)} %copy.21) | data formatting | bytes 1179648 | tf_op jit(solution)/shard_map/all_to_all | solution.py:118
  72.1 0.3 sub.24
  72.5 0.7 multiply_subtract_fusion
  73.1 0.5 pad_maximum_fusion.4
  73.7 0.9 %copy.22 = f32[8,2,12,768]{3,1,2,0:T(2,128)} copy(f32[8,2,12,768]{3,1,0,2:T(2,128)S(1)} %pad_maximum_fusion.4) | data formatting | bytes 1179648 | tf_op jit(solution)/shard_map/stack | solution.py:50
  (12 shorter events, 0.1 us)
Async XLA Ops:
  0.0 8.3 %copy-start.5 = (f32[2,12,768]{2,0,1:T(2,128)S(1)}, f32[2,12,768]{2,0,1:T(2,128)}, u32[]{:S(2)}) copy-start(f32[2,12,768]{2,0,1:T(2,128)} %param.8) | copy-start | bytes 221188
  0.0 8.4 %copy-start = (f32[8,2,12,768]{3,1,2,0:T(2,128)S(1)}, f32[8,2,12,768]{3,1,2,0:T(2,128)}, u32[]{:S(2)}) copy-start(f32[8,2,12,768]{3,1,2,0:T(2,128)} %param.6) | copy-start | bytes 1769476
  1.0 7.9 %collective-permute-start = (f32[9,2,1,768]{3,1,0,2:T(2,128)S(1)}, f32[9,2,1,768]{3,1,0,2:T(2,128)S(1)}, u32[]{:S(2)}, u32[]{:S(2)}) collective-permute-start(f32[9,2,1,768]{3,1,0,2:T(2,128)S(1)} %get-tuple-element.9), channel_id=1, source_target_pairs={{0,1},{1,2},{2,3},{3,4},{4,5},{5,6},{6,7},{7,8},{8,9},{9,10},{10,1... | collective-permute-start | bytes 165896 | tf_op jit(solution)/shard_map/ppermute | solution.py:15
  1.5 7.4 %collective-permute-start.1 = (f32[9,2,1,768]{3,1,0,2:T(2,128)S(1)}, f32[9,2,1,768]{3,1,0,2:T(2,128)S(1)}, u32[]{:S(2)}, u32[]{:S(2)}) collective-permute-start(f32[9,2,1,768]{3,1,0,2:T(2,128)S(1)} %get-tuple-element.10), channel_id=1, source_target_pairs={{1,0},{2,1},{3,2},{4,3},{5,4},{6,5},{7,6},{8,7},{9,8},{10,9},{11,1... | collective-permute-start | bytes 165896 | tf_op jit(solution)/shard_map/ppermute | solution.py:16
  8.4 0.9 %copy-start.3 = (f32[2,12,768]{2,0,1:T(2,128)S(1)}, f32[2,12,768]{2,0,1:T(2,128)}, u32[]{:S(2)}) copy-start(f32[2,12,768]{2,0,1:T(2,128)} %param.7) | copy-start | bytes 221188
  10.5 1.2 %copy-start.1 = (f32[8,2,12,768]{3,1,0,2:T(2,128)}, f32[8,2,12,768]{3,1,0,2:T(2,128)S(1)}, u32[]{:S(2)}) copy-start(f32[8,2,12,768]{3,1,0,2:T(2,128)S(1)} %fusion.6) | copy-start | bytes 1769476
  12.3 7.4 %copy-start.6 = (s32[768]{0:T(1024)S(1)}, s32[768]{0:T(1024)}, u32[]{:S(2)}) copy-start(s32[768]{0:T(1024)} %param.10) | copy-start | bytes 9220
  14.7 20.5 %all-to-all-start = ((f32[16,1,9216]{2,1,0:T(1,128)}), f32[16,1,9216]{2,1,0:T(1,128)S(1)}, u32[]{:S(2)}, u32[]{:S(2)}) async-start(f32[16,1,9216]{2,1,0:T(1,128)} %reshape.72), calls=%async_computation | async-start | bytes 1179648 | tf_op jit(solution)/shard_map/all_to_all | solution.py:107
  44.8 6.8 %copy-start.4 = (f32[1,12,768]{2,0,1:T(1,128)S(1)}, f32[1,12,768]{2,0,1:T(1,128)}, u32[]{:S(2)}) copy-start(f32[1,12,768]{2,0,1:T(1,128)} %param.9) | copy-start | bytes 110596
  47.2 20.0 %all-to-all-start.1 = ((f32[16,1,9216]{2,1,0:T(1,128)}), f32[16,1,9216]{2,1,0:T(1,128)S(1)}, u32[]{:S(2)}, u32[]{:S(2)}) async-start(f32[16,1,9216]{2,1,0:T(1,128)} %reshape.74), calls=%async_computation.1 | async-start | bytes 1179648 | tf_op jit(solution)/shard_map/all_to_all | solution.py:118
  70.8 1.3 %copy-start.2 = (f32[8,2,12,768]{3,1,0,2:T(2,128)S(1)}, f32[8,2,12,768]{3,1,0,2:T(2,128)}, u32[]{:S(2)}) copy-start(f32[8,2,12,768]{3,1,0,2:T(2,128)} %copy-done.1) | copy-start | bytes 1769476
